TPU v7x, 32 devices: a whole 2x2x4 slice. The times are simulated.
32 devices in a mesh: section: 2 (over core), expert: 8 (over z, x), tensor: 2 (over y).
Axes of the slice: x: 2, y: 2, z: 4, core: 2. Of those that a mesh axis runs over, the one named last changes fastest.
Arguments:
- sent: bfloat16 [2, 256, 4096], P('section', ('expert', 'tensor')), may hold values from -20 to 20
- norm_gain: float32 [2, 4096], P('section'), may hold values from 0.1 to 1.9
- router: bfloat16 [2, 4096, 8], P('section'), may hold values from -0.09375 to 0.09375
- w_in: bfloat16 [2, 8, 4096, 2048], P('section', 'expert', None, 'tensor'), may hold values from -0.09375 to 0.09375
- w_out: bfloat16 [2, 8, 2048, 4096], P('section', 'expert', 'tensor'), may hold values from -0.125 to 0.125
- expert_ids: int32 [2, 256, 2], P('section', ('expert', 'tensor')), may hold values from 0 to 7, as said below
Outputs:
- handed: bfloat16 [2, 256, 4096], P('section', ('expert', 'tensor'))
Inputs may be any that keep to these rules, and one draw needn't show every extreme that they name: `expert_ids`: each token names two different experts of the 8.
All inputs are finite; a program needn't handle non-finite values.
Results may differ from a plain program's by a relative error of at most 0.0054.
Values may be sent and summed in bfloat16 or wider, within the bound.
A program may use at most 64 MiB of HBM per device.

v0:
```python
import jax
import jax.numpy as jnp
from jax import lax
from jax.sharding import PartitionSpec as P


def passed_along(value, axis, steps):
    count = lax.axis_size(axis)
    pairs = [(source, (source + steps) % count) for source in range(count)]
    return lax.ppermute(value, axis, pairs)


def normalize(inputs, gain_row):
    widened = inputs.astype(jnp.float32)
    mean_sq = jnp.mean(widened * widened, axis=-1, keepdims=True)
    return (widened * lax.rsqrt(mean_sq + 1e-05) * gain_row).astype(jnp.bfloat16)


def route(normed, router_mat, expert_pick, tok_block, capacity):
    logits = jnp.dot(normed, router_mat, preferred_element_type=jnp.float32)
    experts = router_mat.shape[1]
    labels = jnp.arange(experts, dtype=jnp.int32)
    pair_hot = (expert_pick[:, :, None] == labels[None, None, :]).astype(jnp.float32)
    picked = jnp.sum(pair_hot * logits[:, None, :], axis=-1)
    squashed = jax.nn.sigmoid(picked)
    gate_vals = squashed / jnp.sum(squashed, axis=-1, keepdims=True)
    blocks = expert_pick.shape[0] // tok_block
    pair_order = jnp.transpose(expert_pick.reshape(blocks, tok_block, 2), (0, 2, 1)).reshape(
        blocks, 2 * tok_block
    )
    one_hot = (pair_order[:, :, None] == labels[None, None, :]).astype(jnp.int32)
    before = jnp.cumsum(one_hot, axis=1) - one_hot
    pair_ranks = jnp.sum(before * one_hot, axis=-1)
    pair_ranks = jnp.transpose(pair_ranks.reshape(blocks, 2, tok_block), (0, 2, 1)).reshape(-1, 2)
    is_kept = pair_ranks < capacity
    return (gate_vals, pair_ranks, is_kept)


def on_device(sent, norm_gain, router, w_in, w_out, expert_ids):
    arrived = passed_along(sent, "section", 1)[0]
    tok_count = arrived.shape[0]
    model_width = arrived.shape[1]
    experts = router.shape[2]
    top_count = expert_ids.shape[2]
    n_tensor = lax.axis_size("tensor")
    capacity = max(2, (5 * top_count * tok_count + 4 * experts - 1) // (4 * experts))
    slot_count = experts * capacity
    normed = normalize(arrived, norm_gain[0])
    expert_pick = expert_ids[0]
    gate_vals, pair_ranks, is_kept = route(normed, router[0], expert_pick, tok_count, capacity)
    slot_ids = expert_pick * capacity + pair_ranks
    slot_labels = jnp.arange(slot_count, dtype=jnp.int32)
    slot_hot = ((slot_ids[:, :, None] == slot_labels[None, None, :]) & is_kept[:, :, None]).astype(
        jnp.float32
    )
    placement = jnp.transpose(jnp.sum(slot_hot, axis=1)).astype(jnp.bfloat16)
    combine_mat = jnp.sum(slot_hot * gate_vals[:, :, None], axis=1)
    send_rows = jnp.dot(placement, normed, preferred_element_type=jnp.float32).astype(jnp.bfloat16)
    w_first = w_in[0, 0]
    w_second = w_out[0, 0]
    grouped = lax.all_gather(send_rows[None], "tensor", axis=0, tiled=True)
    slot_grid = grouped.reshape(n_tensor, experts, capacity, model_width)
    received = lax.all_to_all(slot_grid, "expert", split_axis=1, concat_axis=1, tiled=True)
    hidden = jax.nn.gelu(
        jnp.dot(received.reshape(-1, model_width), w_first, preferred_element_type=jnp.float32)
    ).astype(jnp.bfloat16)
    summed = lax.psum_scatter(
        jnp.dot(hidden, w_second, preferred_element_type=jnp.float32).astype(jnp.bfloat16),
        "tensor",
        scatter_dimension=0,
        tiled=True,
    )
    returned = lax.all_to_all(summed, "expert", split_axis=0, concat_axis=0, tiled=True)
    combined = arrived.astype(jnp.float32) + jnp.dot(
        combine_mat, returned.astype(jnp.float32), precision=lax.Precision.HIGHEST
    )
    return passed_along(combined.astype(jnp.bfloat16)[None], "section", 1)


def solution(mesh):
    return jax.shard_map(
        on_device,
        mesh=mesh,
        in_specs=(
            P("section", ("expert", "tensor"), None),
            P("section", None),
            P("section", None, None),
            P("section", "expert", None, "tensor"),
            P("section", "expert", "tensor", None),
            P("section", ("expert", "tensor"), None),
        ),
        out_specs=P("section", ("expert", "tensor"), None),
        check_vma=False,
    )
```

profile of v0, /device:TPU:1, one launch (start us, length us, event | category | flops | bytes accessed | tf_op | source)
XLA Modules:
  0.0 103.0 jit_solution(10744398580045776437)
XLA Ops:
  6.5 0.0 copy-start
  6.5 0.0 reduce-scatter.2.cloned.1.call-start
  6.5 0.1 collective-permute-start
  6.6 0.8 eq.53
  7.4 0.1 fusion.43
  7.4 0.1 reduce_window_sum.11
  7.5 0.2 select_reduce_fusion.1
  7.7 0.1 reshape.170
  7.8 0.7 bitcast_add_fusion
  8.4 0.0 collective-permute-done
  8.5 0.1 fusion.25
  8.6 0.0 copy-done
  8.6 0.9 fusion.35
  9.6 0.7 select_reduce_fusion.2
  10.3 0.1 convert_reduce_fusion
  10.4 1.0 convolution_convert_fusion
  11.4 11.4 %all-gather = bf16[80,4096]{1,0:T(8,128)(2,1)S(1)} all-gather(bf16[40,4096]{1,0:T(8,128)(2,1)S(1)} %convolution_convert_fusion), channel_id=2, replica_groups=mesh['section'=2,'expert'=8,'tensor'=2] {'tensor'}, dimensions={0}, use_global_device_ids=true | all-gather | bytes 983040 | tf_op jit(solution)/shard_map/all_gather | solution.py:61
  22.8 0.3 reshape.172
  23.1 0.7 copy.21
  23.9 21.8 %all_to_all.17 = bf16[2,8,5,4096]{3,0,2,1:T(2,128)(2,1)S(1)} all-to-all(bf16[2,8,5,4096]{3,0,2,1:T(2,128)(2,1)S(1)} %copy.21), channel_id=1, replica_groups=mesh['section'=2,'expert'=8,'tensor'=2] {'expert'}, dimensions={1} | all-to-all | bytes 1310720 | tf_op jit(solution)/shard_map/all_to_all | solution.py:63
  45.7 0.4 copy.22
  46.1 0.3 reshape.173
  46.3 9.7 %fusion.4 = bf16[80,4096]{1,0:T(8,128)(2,1)} fusion(bf16[1,1,1024,4096]{3,2,1,0:T(8,128)(2,1)} %param.10, bf16[80,4096]{1,0:T(8,128)(2,1)S(1)} %reshape.173, bf16[1,1,4096,1024]{3,2,1,0:T(8,128)(2,1)} %param.9), kind=kOutput, calls=%fused_computation.4 | convolution fusion | flops 1343242240 | bytes 18087936 | tf_op jit(solution)/shard_map/dot_general | solution.py:68
  56.0 0.0 reduce-scatter.2.cloned.1.call-update
  56.1 16.3 %reduce-scatter.2.cloned.1.call-done = bf16[40,4096]{1,0:T(8,128)(2,1)} async-done(((bf16[80,4096]{1,0:T(8,128)(2,1)}), bf16[40,4096]{1,0:T(8,128)(2,1)}) %reduce-scatter.2.cloned.1.call-update) | async-done | bytes 327696 | tf_op jit(solution)/shard_map/reduce_scatter | solution.py:67
  72.4 1.1 %all_to_all.12 = bf16[8,5,4096]{2,1,0:T(8,128)(2,1)S(1)} reshape(bf16[40,4096]{1,0:T(8,128)(2,1)} %reduce-scatter.2.cloned.1.call-done) | data formatting | bytes 655360 | tf_op jit(solution)/shard_map/all_to_all | solution.py:73
  73.5 18.7 %all_to_all.18 = bf16[8,5,4096]{2,1,0:T(8,128)(2,1)S(1)} all-to-all(bf16[8,5,4096]{2,1,0:T(8,128)(2,1)S(1)} %all_to_all.12), channel_id=1, replica_groups=mesh['section'=2,'expert'=8,'tensor'=2] {'expert'}, dimensions={0} | all-to-all | bytes 655360 | tf_op jit(solution)/shard_map/all_to_all | solution.py:73
  92.2 0.1 all_to_all.14
  92.4 0.3 fusion.8
  92.7 1.9 %collective-permute-start.1 = (bf16[1,16,4096]{2,1,0:T(8,128)(2,1)S(1)}, bf16[1,16,4096]{2,1,0:T(8,128)(2,1)S(1)}, u32[]{:S(2)}, u32[]{:S(2)}) collective-permute-start(bf16[1,16,4096]{2,1,0:T(8,128)(2,1)S(1)} %fusion.8), channel_id=1, source_target_pairs={{0,16},{16,0},{1,17},{17,1},{2,18},{18,2},{3,19},{19,3},{4,20},{20... | collective-permute-start | bytes 393224 | tf_op jit(solution)/shard_map/ppermute | solution.py:10
  94.5 1.0 collective-permute-done.1
  95.5 0.7 copy.24
  (4 shorter events, 0.1 us)
Async XLA Ops:
  6.5 2.1 %copy-start = (bf16[1,4096,8]{1,2,0:T(8,128)(2,1)S(1)}, bf16[1,4096,8]{1,2,0:T(8,128)(2,1)}, u32[]{:S(2)}) copy-start(bf16[1,4096,8]{1,2,0:T(8,128)(2,1)} %param.8) | copy-start | bytes 196612
  6.5 65.9 %reduce-scatter.2.cloned.1.call-start = ((), (), s32[]{:S(2)}) async-start(), calls=%async_computation.3 | async-start | bytes 983040 | tf_op jit(solution)/shard_map/reduce_scatter | solution.py:67
  6.5 1.9 %collective-permute-start = (bf16[1,16,4096]{2,1,0:T(8,128)(2,1)}, bf16[1,16,4096]{2,1,0:T(8,128)(2,1)S(1)}, u32[]{:S(2)}, u32[]{:S(2)}) collective-permute-start(bf16[1,16,4096]{2,1,0:T(8,128)(2,1)} %param.6), channel_id=1, source_target_pairs={{0,16},{16,0},{1,17},{17,1},{2,18},{18,2},{3,19},{19,3},{4,20},{20... | collective-permute-start | bytes 393224 | tf_op jit(solution)/shard_map/ppermute | solution.py:10
  92.7 2.9 %collective-permute-start.1 = (bf16[1,16,4096]{2,1,0:T(8,128)(2,1)S(1)}, bf16[1,16,4096]{2,1,0:T(8,128)(2,1)S(1)}, u32[]{:S(2)}, u32[]{:S(2)}) collective-permute-start(bf16[1,16,4096]{2,1,0:T(8,128)(2,1)S(1)} %fusion.8), channel_id=1, source_target_pairs={{0,16},{16,0},{1,17},{17,1},{2,18},{18,2},{3,19},{19,3},{4,20},{20... | collective-permute-start | bytes 393224 | tf_op jit(solution)/shard_map/ppermute | solution.py:10
Sparse Core Ops, SparseCore 0:
  56.2 16.1 reduce-scatter.1
where the time goes:
time: 104 us; the launch traced here: 103 us
  blocking collectives  51.9 us (50%)
  waiting for transfers between devices  17.3 us (17%)
  between operations  13.5 us (13%)
  matrix products  11.9 us (11%)
  local copies, waits for them, and re-layouts  4.42 us (4%)
  other arithmetic  2 us (2%)
  starting transfers between devices  1.93 us (2%)
    all_to_all x1, blocking collectives, on_device(): lax.all_to_all(slot_grid, 'expert', split_axis=1, concat_axis=1, tiled=True)  21.8 us
    all_to_all x1, blocking collectives, on_device(): lax.all_to_all(summed, 'expert', split_axis=0, concat_axis=0, tiled=True)  18.7 us
    reduce_scatter x1, waiting for transfers between devices, on_device(): lax.psum_scatter(jnp.dot(hidden, w_second, preferred_element_type=jnp.flo...  16.3 us
    all_gather x1, blocking collectives, on_device(): grouped = lax.all_gather(send_rows[None], 'tensor', axis=0, tiled=True)  11.4 us
    dot_general x1, matrix products, on_device(): jnp.dot(hidden, w_second, preferred_element_type=jnp.float32)  9.7 us
  transfers between devices with their start and end apart: 3, of which 2 were waited for; matrix products, arithmetic and copies ran while one was open for 2% of the time, Pallas kernels for 0%

commit v1 on v0

v1 whole, which is shorter than its diff:
```python
import functools

import jax
import jax.numpy as jnp
from jax import lax
from jax.experimental import pallas as pl
from jax.experimental.pallas import tpu as pltpu
from jax.sharding import PartitionSpec as P

MESH = pl.DeviceIdType.MESH
F32 = jnp.float32
BF16 = jnp.bfloat16
LANES = 128


def kernel(
    n_expert, n_tensor, cap, tok,
    x_ref, gain_slab, gain_row, router_t, ids_ref, w1_hbm, w2_hbm,
    out_ref,
    w1, w2, pad_ids, meta_send, meta_recv, aux_send, aux_recv, logit_pad,
    gathered, disp, got, flat, lhs, hid, partial, part_send, part_recv, ret_send, ret_recv, back,
    w_sem, meta_sem, aux_sem, disp_ss, disp_rs, fwd_ss, fwd_rs, part_ss, part_rs, ret_ss, ret_rs,
):
    core, e, t = lax.axis_index("section"), lax.axis_index("expert"), lax.axis_index("tensor")
    peer = 1 - core
    width = x_ref.shape[1]
    chunks = width // LANES
    half = chunks // 2
    slots = n_expert * cap
    mine = slots
    rows = n_tensor * slots
    ff = w1.shape[1]

    load1 = pltpu.make_async_copy(w1_hbm, w1, w_sem.at[0])
    load2 = pltpu.make_async_copy(w2_hbm, w2, w_sem.at[1])
    load1.start()
    load2.start()

    barrier = pltpu.get_barrier_semaphore()

    def greet(i, carry):
        pl.semaphore_signal(
            barrier, inc=1, device_id=(peer, lax.rem(e + i, n_expert), t), device_id_type=MESH
        )
        return carry

    lax.fori_loop(0, n_expert, greet, 0)
    for d in range(1, n_tensor):
        pl.semaphore_signal(
            barrier, inc=1, device_id=(core, e, lax.rem(t + d, n_tensor)), device_id_type=MESH
        )

    pad_ids[...] = jnp.full(pad_ids.shape, -1, jnp.int32)
    pad_ids[0:2, 0:tok] = ids_ref[...]
    label_rows = max(16, n_expert)
    labels = lax.broadcasted_iota(jnp.int32, (label_rows, LANES), 0)
    hot = [(labels == pad_ids[k:k + 1, :]) for k in range(2)]
    hot_f = [jnp.where(h, 1.0, 0.0).astype(F32) for h in hot]
    earlier = jnp.where(
        lax.broadcasted_iota(jnp.int32, (LANES, LANES), 0)
        < lax.broadcasted_iota(jnp.int32, (LANES, LANES), 1), 1.0, 0.0
    ).astype(BF16)
    before = [jnp.dot(h.astype(BF16), earlier, preferred_element_type=F32) for h in hot_f]
    before[1] = before[1] + jnp.sum(hot_f[0], axis=1, keepdims=True)
    meta_send[...] = pad_ids[...]
    for k in range(2):
        rank = jnp.sum(hot_f[k] * before[k], axis=0, keepdims=True).astype(jnp.int32)
        pick = pad_ids[k:k + 1, :]
        kept = jnp.logical_and(rank < cap, pick >= 0)
        meta_send[2 + k:3 + k, :] = jnp.where(kept, pick * cap + rank, -1)
    aux_send[0:n_expert, :] = router_t[...].astype(F32)
    aux_send[n_expert:n_expert + 8, :] = jnp.broadcast_to(gain_row[...], (8, width))

    pl.semaphore_wait(barrier, n_expert + n_tensor - 1)

    meta_copy = pltpu.make_async_remote_copy(
        meta_send, meta_recv, meta_sem.at[0], meta_sem.at[1], device_id=(peer, e, t), device_id_type=MESH
    )
    meta_copy.start()
    aux_copy = pltpu.make_async_remote_copy(
        aux_send, aux_recv, aux_sem.at[0], aux_sem.at[1], device_id=(peer, e, t), device_id_type=MESH
    )
    meta_copy.wait()
    aux_copy.start()

    slot_rows = back.shape[0] // half
    slot_labels = lax.broadcasted_iota(jnp.int32, (LANES, LANES), 0)
    place = [slot_labels == meta_recv[2 + k:3 + k, :] for k in range(2)]
    place_f = [jnp.where(m, 1.0, 0.0).astype(F32) for m in place]
    spread = (place_f[0] + place_f[1])[0:slot_rows, 0:tok].astype(BF16)
    rows_f = jnp.dot(spread, x_ref[...], preferred_element_type=F32)
    for c in range(chunks):
        gathered[pl.ds(c, slots, stride=chunks), :] = rows_f[0:slots, c * LANES:(c + 1) * LANES]
    disp[...] = gathered[...].reshape(disp.shape).astype(BF16)

    def disp_copy(i, sending):
        target = lax.rem(e + i, n_expert)
        return pltpu.make_async_remote_copy(
            disp.at[target], got.at[0, lax.rem(n_expert - i, n_expert) if sending else i],
            disp_ss.at[i], disp_rs.at[lax.rem(n_expert - i, n_expert) if sending else i],
            device_id=(peer, target, t), device_id_type=MESH,
        )

    def fwd_copy(d, i, sending):
        there = (n_tensor - d) if sending else d
        return pltpu.make_async_remote_copy(
            got.at[0, i], got.at[there, i], fwd_ss.at[d, i], fwd_rs.at[there, i],
            device_id=(core, e, lax.rem(t + d, n_tensor)), device_id_type=MESH,
        )

    def send_disp(i, carry):
        disp_copy(i, True).start()
        return carry

    lax.fori_loop(0, n_expert, send_disp, 0)

    def normalise(d, i):
        piece = got[d, i].astype(F32).reshape(cap, chunks, LANES)
        total = jnp.sum(jnp.sum(piece * piece, axis=1, keepdims=True), axis=2, keepdims=True)
        scale = lax.rsqrt(total * (1.0 / width) + 1e-05)
        normed = (piece * scale * gain_slab[...][None]).astype(BF16).astype(F32)
        start = pl.multiple_of((d * n_expert + i) * (cap * chunks), cap * chunks)
        flat[pl.ds(start, cap * chunks), :] = normed.reshape(cap * chunks, LANES)

    def take(i, carry):
        disp_copy(i, False).wait_recv()
        for d in range(1, n_tensor):
            fwd_copy(d, i, True).start()
        normalise(0, i)
        return carry

    lax.fori_loop(0, n_expert, take, 0)
    for d in range(1, n_tensor):
        def take_fwd(i, carry, d=d):
            fwd_copy(d, i, False).wait_recv()
            normalise(d, i)
            return carry

        lax.fori_loop(0, n_expert, take_fwd, 0)

    for c in range(chunks):
        lhs[:, c * LANES:(c + 1) * LANES] = flat[pl.ds(c, rows, stride=chunks), :].astype(BF16)

    tile = 256
    load1.wait()

    def first(n, carry):
        cols = pl.ds(pl.multiple_of(n * tile, tile), tile)
        value = jnp.dot(lhs[...], w1[:, cols], preferred_element_type=F32)
        hid[:, cols] = jax.nn.gelu(value).astype(BF16)
        return carry

    lax.fori_loop(0, ff // tile, first, 0)
    load2.wait()

    def part_copy(h, d, sending):
        there = (n_tensor - d) if sending else d
        return pltpu.make_async_remote_copy(
            part_send.at[h, d], part_recv.at[h, there], part_ss.at[h, d], part_rs.at[h, there],
            device_id=(core, e, lax.rem(t + d, n_tensor)), device_id_type=MESH,
        )

    def ret_copy(h, i, sending):
        target = lax.rem(e + i, n_expert)
        where = e if sending else target
        return pltpu.make_async_remote_copy(
            ret_send.at[h, i], ret_recv.at[h, where], ret_ss.at[h, i], ret_rs.at[h, where],
            device_id=(peer, target, t), device_id_type=MESH,
        )

    piece_rows = mine * half

    for h in range(2):
        def second(n, carry, h=h):
            cols = pl.ds(pl.multiple_of(h * half * LANES + n * tile, tile), tile)
            value = jnp.dot(hid[...], w2[:, cols], preferred_element_type=F32)
            for j in range(tile // LANES):
                partial[h, pl.ds(n * (tile // LANES) + j, rows, stride=half), :] = (
                    value[:, j * LANES:(j + 1) * LANES]
                )
            return carry

        lax.fori_loop(0, half * LANES // tile, second, 0)
        for d in range(1, n_tensor):
            part_send[h, d] = partial[h, d * piece_rows:(d + 1) * piece_rows, :].astype(BF16)
            part_copy(h, d, True).start()

    def reduce(h):
        total = partial[h, 0:piece_rows, :].astype(BF16).astype(F32)
        for d in range(1, n_tensor):
            part_copy(h, d, False).wait_recv()
            total = total + part_recv[h, d].astype(F32)
        ret_send[h] = total.astype(BF16).reshape(n_expert, cap * half, LANES)

        def send(i, carry):
            ret_copy(h, i, True).start()
            return carry

        lax.fori_loop(0, n_expert, send, 0)

    reduce(0)
    reduce(1)

    aux_copy.wait()
    x_f = x_ref[...].astype(F32)
    mean_sq = jnp.mean(x_f * x_f, axis=-1, keepdims=True)
    normed = (x_f * lax.rsqrt(mean_sq + 1e-05) * aux_recv[n_expert:n_expert + 1, :]).astype(BF16)
    logit_pad[...] = jnp.zeros(logit_pad.shape, F32)
    logit_pad[0:n_expert, 0:tok] = lax.dot_general(
        aux_recv[0:n_expert, :].astype(BF16), normed, (((1,), (1,)), ((), ())), preferred_element_type=F32
    )
    squashed = []
    for k in range(2):
        hit = labels == meta_recv[k:k + 1, :]
        squashed.append(
            jax.nn.sigmoid(jnp.sum(jnp.where(hit, logit_pad[...], 0.0), axis=0, keepdims=True))
        )
    both = squashed[0] + squashed[1]
    weights = place_f[0] * (squashed[0] / both) + place_f[1] * (squashed[1] / both)
    combine = jnp.transpose(weights)[0:tok, 0:slot_rows]
    high = combine.astype(BF16)
    rest = combine - high.astype(F32)
    mid = rest.astype(BF16)
    low = (rest - mid.astype(F32)).astype(BF16)
    if slot_rows > slots:
        back[slots * half:slot_rows * half, :] = jnp.zeros(((slot_rows - slots) * half, LANES), F32)

    for h in range(2):
        def arrive(i, carry, h=h):
            ret_copy(h, i, False).wait_recv()
            return carry

        lax.fori_loop(0, n_expert, arrive, 0)
        back[0:slots * half, :] = ret_recv[h].reshape(slots * half, LANES).astype(F32)
        table = jnp.concatenate(
            [back[pl.ds(c, slot_rows, stride=half), :].astype(BF16) for c in range(half)], axis=1
        )
        cols = slice(h * half * LANES, (h + 1) * half * LANES)
        added = jnp.dot(high, table, preferred_element_type=F32)
        added = added + jnp.dot(mid, table, preferred_element_type=F32)
        added = added + jnp.dot(low, table, preferred_element_type=F32)
        out_ref[:, cols] = (x_ref[:, cols].astype(F32) + added).astype(BF16)

    def drain(i, carry):
        disp_copy(i, True).wait_send()
        for d in range(1, n_tensor):
            fwd_copy(d, i, True).wait_send()
        for h in range(2):
            ret_copy(h, i, True).wait_send()
        return carry

    lax.fori_loop(0, n_expert, drain, 0)
    for h in range(2):
        for d in range(1, n_tensor):
            part_copy(h, d, True).wait_send()


def on_device(sent, norm_gain, router, w_in, w_out, expert_ids):
    tok, width = sent.shape[1], sent.shape[2]
    n_expert, n_tensor = lax.axis_size("expert"), lax.axis_size("tensor")
    top = expert_ids.shape[2]
    ff = w_in.shape[3]
    cap = max(2, (5 * top * tok + 4 * n_expert - 1) // (4 * n_expert))
    slots = n_expert * cap
    slot_rows = -(-slots // 16) * 16
    rows = n_tensor * slots
    chunks = width // LANES
    half = chunks // 2
    vmem = pl.BlockSpec(memory_space=pltpu.VMEM)
    hbm = pl.BlockSpec(memory_space=pl.ANY)
    dma = pltpu.SemaphoreType.DMA
    result = pl.pallas_call(
        functools.partial(kernel, n_expert, n_tensor, cap, tok),
        out_shape=jax.ShapeDtypeStruct((tok, width), BF16),
        in_specs=[vmem, vmem, vmem, vmem, vmem, hbm, hbm],
        out_specs=vmem,
        scratch_shapes=[
            pltpu.VMEM((width, ff), BF16),
            pltpu.VMEM((ff, width), BF16),
            pltpu.VMEM((8, LANES), jnp.int32),
            pltpu.VMEM((8, LANES), jnp.int32),
            pltpu.VMEM((8, LANES), jnp.int32),
            pltpu.VMEM((n_expert + 8, width), F32),
            pltpu.VMEM((n_expert + 8, width), F32),
            pltpu.VMEM((max(16, n_expert), LANES), F32),
            pltpu.VMEM((slots * chunks, LANES), F32),
            pltpu.VMEM((n_expert, cap * chunks, LANES), BF16),
            pltpu.VMEM((n_tensor, n_expert, cap * chunks, LANES), BF16),
            pltpu.VMEM((rows * chunks, LANES), F32),
            pltpu.VMEM((rows, width), BF16),
            pltpu.VMEM((rows, ff), BF16),
            pltpu.VMEM((2, rows * half, LANES), F32),
            pltpu.VMEM((2, n_tensor, slots * half, LANES), BF16),
            pltpu.VMEM((2, n_tensor, slots * half, LANES), BF16),
            pltpu.VMEM((2, n_expert, cap * half, LANES), BF16),
            pltpu.VMEM((2, n_expert, cap * half, LANES), BF16),
            pltpu.VMEM((slot_rows * half, LANES), F32),
            dma((2,)),
            dma((2,)),
            dma((2,)),
            dma((n_expert,)),
            dma((n_expert,)),
            dma((n_tensor, n_expert)),
            dma((n_tensor, n_expert)),
            dma((2, n_tensor)),
            dma((2, n_tensor)),
            dma((2, n_expert)),
            dma((2, n_expert)),
        ],
        compiler_params=pltpu.CompilerParams(
            collective_id=0, has_side_effects=True, vmem_limit_bytes=56 * 2**20
        ),
        name="expert_layer",
    )(
        sent[0],
        norm_gain.reshape(chunks, LANES),
        norm_gain,
        jnp.transpose(router[0]),
        jnp.transpose(expert_ids[0]),
        w_in[0, 0],
        w_out[0, 0],
    )
    return result[None]


def solution(mesh):
    return jax.shard_map(
        on_device,
        mesh=mesh,
        in_specs=(
            P("section", ("expert", "tensor"), None),
            P("section", None),
            P("section", None, None),
            P("section", "expert", None, "tensor"),
            P("section", "expert", "tensor", None),
            P("section", ("expert", "tensor"), None),
        ),
        out_specs=P("section", ("expert", "tensor"), None),
        check_vma=False,
    )
```

time: 104 us -> 45.8 us (0.44)
  blocking collectives: 51.9 us -> 0 us
  Pallas kernels: 0 us -> 44.1 us
  waiting for transfers between devices: 17.3 us -> 0 us
  between operations: 13.5 us -> 0.01 us
  matrix products: 11.9 us -> 0 us
  local copies, waits for them, and re-layouts: 4.42 us -> 1.57 us
  other arithmetic: 2 us -> 0 us
  starting transfers between devices: 1.93 us -> 0 us
    pallas_call x0 -> x1, Pallas kernels: none -> 44.1 us  [on_device(): pl.pallas_call(functools.partial(kernel, n_expert, n_tensor, cap, tok), o...]
    all_to_all x2 -> x0, blocking collectives: 40.5 us -> none  [the longest x1 21.8 us: on_device(): lax.all_to_all(slot_grid, 'expert', split_axis=1, concat_axis=1, tiled=True)]
    reduce_scatter x1 -> x0, waiting for transfers between devices: 16.3 us -> none  [on_device(): lax.psum_scatter(jnp.dot(hidden, w_second, preferred_element_type=jnp.flo...]
    dot_general x4 -> x0, matrix products: 11.9 us -> none  [the longest x1 9.7 us: on_device(): jnp.dot(hidden, w_second, preferred_element_type=jnp.float32)]
    all_gather x1 -> x0, blocking collectives: 11.4 us -> none  [on_device(): grouped = lax.all_gather(send_rows[None], 'tensor', axis=0, tiled=True)]
    ppermute x2 -> x0, starting transfers between devices: 1.93 us -> none  [passed_along(): return lax.ppermute(value, axis, pairs)]
    all_to_all x3 -> x0, local copies, waits for them, and re-layouts: 1.63 us -> none  [the longest x2 1.25 us: on_device(): lax.all_to_all(summed, 'expert', split_axis=0, concat_axis=0, tiled=True)]
    reshape x4 -> x0, local copies, waits for them, and re-layouts: 1.38 us -> none  [the longest x2 1.01 us: on_device(): slot_grid = grouped.reshape(n_tensor, experts, capacity, model_width)]
  transfers between devices with their start and end apart: 3 -> 0, of which waited for: 2 -> 0; matrix products, arithmetic and copies ran while one was open for 2% -> 0% of each run, Pallas kernels for 0% -> 0%
where the time goes in v1:
time: 45.8 us; the launch traced here: 45.6 us
  Pallas kernels  44.1 us (96%)
  local copies, waits for them, and re-layouts  1.57 us (3%)
    pallas_call x1, Pallas kernels, on_device(): pl.pallas_call(functools.partial(kernel, n_expert, n_tensor, cap, tok), o...  44.1 us
    unnamed x1, local copies, waits for them, and re-layouts  1.57 us

profile of v1, /device:TPU:1, one launch (start us, length us, event | category | flops | bytes accessed | tf_op | source)
XLA Modules:
  0.0 45.6 jit_solution(3185352798560290280)
XLA Ops:
  0.0 44.1 %expert_layer.1 = bf16[16,4096]{1,0:T(8,128)(2,1)} custom-call(bf16[16,4096]{1,0:T(8,128)(2,1)} %bitcast.14, f32[32,128]{1,0:T(8,128)} %bitcast.16, f32[1,4096]{1,0:T(1,128)} %gain_row.1, bf16[8,4096]{1,0:T(8,128)(2,1)} %bitcast.15, s32[2,16]{1,0:T(2,128)} %bitcast.17, bf16[4096,1024]{1,0:T(8,128)(2,1)} %bitcast.11, bf16[1024,4096]{1,0:T(8,128)(2,1)} %bitcast.12), custom_call_target="tpu_custom_call" | custom-call | tf_op jit(solution)/shard_map/expert_layer/pallas_call | solution.py:272
  44.1 1.6 %copy.8 = bf16[1,16,4096]{2,1,0:T(8,128)(2,1)} copy(bf16[1,16,4096]{2,1,0:T(8,128)(2,1)} %bitcast.13) | data formatting | bytes 262144

commit v2 on v1

--- a/solution.py
+++ b/solution.py
@@ -11,6 +11,14 @@
 F32 = jnp.float32
 BF16 = jnp.bfloat16
 LANES = 128
+
+
+def flip(index, mask, count):
+    total, bit = 0, 1
+    while bit < count:
+        total = total + lax.rem(index // bit + mask // bit, 2) * bit
+        bit *= 2
+    return total
 
 
 def kernel(
@@ -27,7 +35,6 @@
     chunks = width // LANES
     half = chunks // 2
     slots = n_expert * cap
-    mine = slots
     rows = n_tensor * slots
     ff = w1.shape[1]
 
@@ -93,11 +100,10 @@
         gathered[pl.ds(c, slots, stride=chunks), :] = rows_f[0:slots, c * LANES:(c + 1) * LANES]
     disp[...] = gathered[...].reshape(disp.shape).astype(BF16)
 
-    def disp_copy(i, sending):
-        target = lax.rem(e + i, n_expert)
+    def disp_copy(i):
+        target = flip(e, i, n_expert)
         return pltpu.make_async_remote_copy(
-            disp.at[target], got.at[0, lax.rem(n_expert - i, n_expert) if sending else i],
-            disp_ss.at[i], disp_rs.at[lax.rem(n_expert - i, n_expert) if sending else i],
+            disp.at[target], got.at[0, i], disp_ss.at[i], disp_rs.at[i],
             device_id=(peer, target, t), device_id_type=MESH,
         )
 
@@ -109,7 +115,7 @@
         )
 
     def send_disp(i, carry):
-        disp_copy(i, True).start()
+        disp_copy(i).start()
         return carry
 
     lax.fori_loop(0, n_expert, send_disp, 0)
@@ -123,7 +129,7 @@
         flat[pl.ds(start, cap * chunks), :] = normed.reshape(cap * chunks, LANES)
 
     def take(i, carry):
-        disp_copy(i, False).wait_recv()
+        disp_copy(i).wait_recv()
         for d in range(1, n_tensor):
             fwd_copy(d, i, True).start()
         normalise(0, i)
@@ -153,22 +159,22 @@
     lax.fori_loop(0, ff // tile, first, 0)
     load2.wait()
 
-    def part_copy(h, d, sending):
+    def part_copy(h, d, i, sending):
         there = (n_tensor - d) if sending else d
         return pltpu.make_async_remote_copy(
-            part_send.at[h, d], part_recv.at[h, there], part_ss.at[h, d], part_rs.at[h, there],
+            part_send.at[h, d, i], part_recv.at[h, there, i], part_ss.at[h, d, i], part_rs.at[h, there, i],
             device_id=(core, e, lax.rem(t + d, n_tensor)), device_id_type=MESH,
         )
 
     def ret_copy(h, i, sending):
-        target = lax.rem(e + i, n_expert)
+        target = flip(e, i, n_expert)
         where = e if sending else target
         return pltpu.make_async_remote_copy(
             ret_send.at[h, i], ret_recv.at[h, where], ret_ss.at[h, i], ret_rs.at[h, where],
             device_id=(peer, target, t), device_id_type=MESH,
         )
 
-    piece_rows = mine * half
+    piece_rows = cap * half
 
     for h in range(2):
         def second(n, carry, h=h):
@@ -182,21 +188,28 @@
 
         lax.fori_loop(0, half * LANES // tile, second, 0)
         for d in range(1, n_tensor):
-            part_send[h, d] = partial[h, d * piece_rows:(d + 1) * piece_rows, :].astype(BF16)
-            part_copy(h, d, True).start()
+            def send_part(k, carry, h=h, d=d):
+                i = n_expert - 1 - k
+                start = pl.multiple_of((d * n_expert + i) * piece_rows, piece_rows)
+                part_send[h, d, i] = partial[h, pl.ds(start, piece_rows), :].astype(BF16)
+                part_copy(h, d, i, True).start()
+                return carry
+
+            lax.fori_loop(0, n_expert, send_part, 0)
 
     def reduce(h):
-        total = partial[h, 0:piece_rows, :].astype(BF16).astype(F32)
-        for d in range(1, n_tensor):
-            part_copy(h, d, False).wait_recv()
-            total = total + part_recv[h, d].astype(F32)
-        ret_send[h] = total.astype(BF16).reshape(n_expert, cap * half, LANES)
-
-        def send(i, carry):
+        def one(k, carry):
+            i = n_expert - 1 - k
+            start = pl.multiple_of(i * piece_rows, piece_rows)
+            total = partial[h, pl.ds(start, piece_rows), :].astype(BF16).astype(F32)
+            for d in range(1, n_tensor):
+                part_copy(h, d, i, False).wait_recv()
+                total = total + part_recv[h, d, i].astype(F32)
+            ret_send[h, i] = total.astype(BF16)
             ret_copy(h, i, True).start()
             return carry
 
-        lax.fori_loop(0, n_expert, send, 0)
+        lax.fori_loop(0, n_expert, one, 0)
 
     reduce(0)
     reduce(1)
@@ -242,17 +255,16 @@
         out_ref[:, cols] = (x_ref[:, cols].astype(F32) + added).astype(BF16)
 
     def drain(i, carry):
-        disp_copy(i, True).wait_send()
+        disp_copy(i).wait_send()
         for d in range(1, n_tensor):
             fwd_copy(d, i, True).wait_send()
         for h in range(2):
             ret_copy(h, i, True).wait_send()
+            for d in range(1, n_tensor):
+                part_copy(h, d, i, True).wait_send()
         return carry
 
     lax.fori_loop(0, n_expert, drain, 0)
-    for h in range(2):
-        for d in range(1, n_tensor):
-            part_copy(h, d, True).wait_send()
 
 
 def on_device(sent, norm_gain, router, w_in, w_out, expert_ids):
@@ -290,8 +302,8 @@
             pltpu.VMEM((rows, width), BF16),
             pltpu.VMEM((rows, ff), BF16),
             pltpu.VMEM((2, rows * half, LANES), F32),
-            pltpu.VMEM((2, n_tensor, slots * half, LANES), BF16),
-            pltpu.VMEM((2, n_tensor, slots * half, LANES), BF16),
+            pltpu.VMEM((2, n_tensor, n_expert, cap * half, LANES), BF16),
+            pltpu.VMEM((2, n_tensor, n_expert, cap * half, LANES), BF16),
             pltpu.VMEM((2, n_expert, cap * half, LANES), BF16),
             pltpu.VMEM((2, n_expert, cap * half, LANES), BF16),
             pltpu.VMEM((slot_rows * half, LANES), F32),
@@ -302,8 +314,8 @@
             dma((n_expert,)),
             dma((n_tensor, n_expert)),
             dma((n_tensor, n_expert)),
-            dma((2, n_tensor)),
-            dma((2, n_tensor)),
+            dma((2, n_tensor, n_expert)),
+            dma((2, n_tensor, n_expert)),
             dma((2, n_expert)),
             dma((2, n_expert)),
         ],

time: 45.8 us -> 40.9 us (0.89)
  Pallas kernels: 44.1 us -> 38.9 us
    pallas_call x1, Pallas kernels: 44.1 us -> 38.9 us  [on_device(): pl.pallas_call(functools.partial(kernel, n_expert, n_tensor, cap, tok), o...]
where the time goes in v2:
time: 40.9 us; the launch traced here: 40.4 us
  Pallas kernels  38.9 us (95%)
  local copies, waits for them, and re-layouts  1.57 us (4%)
    pallas_call x1, Pallas kernels, on_device(): pl.pallas_call(functools.partial(kernel, n_expert, n_tensor, cap, tok), o...  38.9 us
    unnamed x1, local copies, waits for them, and re-layouts  1.57 us

profile of v2, /device:TPU:1, one launch (start us, length us, event | category | flops | bytes accessed | tf_op | source)
XLA Modules:
  0.0 40.4 jit_solution(1234316119741652636)
XLA Ops:
  0.0 38.9 %expert_layer.1 = bf16[16,4096]{1,0:T(8,128)(2,1)} custom-call(bf16[16,4096]{1,0:T(8,128)(2,1)} %bitcast.14, f32[32,128]{1,0:T(8,128)} %bitcast.16, f32[1,4096]{1,0:T(1,128)} %gain_row.1, bf16[8,4096]{1,0:T(8,128)(2,1)} %bitcast.15, s32[2,16]{1,0:T(2,128)} %bitcast.17, bf16[4096,1024]{1,0:T(8,128)(2,1)} %bitcast.11, bf16[1024,4096]{1,0:T(8,128)(2,1)} %bitcast.12), custom_call_target="tpu_custom_call" | custom-call | tf_op jit(solution)/shard_map/expert_layer/pallas_call | solution.py:284
  38.9 1.6 %copy.8 = bf16[1,16,4096]{2,1,0:T(8,128)(2,1)} copy(bf16[1,16,4096]{2,1,0:T(8,128)(2,1)} %bitcast.13) | data formatting | bytes 262144

commit v3 on v2

--- a/solution.py
+++ b/solution.py
@@ -23,11 +23,11 @@
 
 def kernel(
     n_expert, n_tensor, cap, tok,
-    x_ref, gain_slab, gain_row, router_t, ids_ref, w1_hbm, w2_hbm,
-    out_ref,
-    w1, w2, pad_ids, meta_send, meta_recv, aux_send, aux_recv, logit_pad,
+    x_hbm, slab_hbm, row_hbm, router_hbm, ids_ref, w1_hbm, w2_hbm,
+    out_hbm,
+    x_ref, gain_slab, gain_row, router_t, out_ref, w1, w2, pad_ids, meta_send, meta_recv, aux_send, aux_recv, logit_pad,
     gathered, disp, got, flat, lhs, hid, partial, part_send, part_recv, ret_send, ret_recv, back,
-    w_sem, meta_sem, aux_sem, disp_ss, disp_rs, fwd_ss, fwd_rs, part_ss, part_rs, ret_ss, ret_rs,
+    in_sem, out_sem, w_sem, meta_sem, aux_sem, disp_ss, disp_rs, fwd_ss, fwd_rs, part_ss, part_rs, ret_ss, ret_rs,
 ):
     core, e, t = lax.axis_index("section"), lax.axis_index("expert"), lax.axis_index("tensor")
     peer = 1 - core
@@ -38,24 +38,32 @@
     rows = n_tensor * slots
     ff = w1.shape[1]
 
+    barrier = pltpu.get_barrier_semaphore()
+
+    def greet(i, carry):
+        pl.semaphore_signal(
+            barrier, inc=1, device_id=(peer, lax.rem(e + i, n_expert), t), device_id_type=MESH
+        )
+        return carry
+
+    lax.fori_loop(0, n_expert, greet, 0)
+    for d in range(1, n_tensor):
+        pl.semaphore_signal(
+            barrier, inc=1, device_id=(core, e, lax.rem(t + d, n_tensor)), device_id_type=MESH
+        )
+
+    small = [
+        pltpu.make_async_copy(src, dst, in_sem.at[n])
+        for n, (src, dst) in enumerate(
+            [(router_hbm, router_t), (row_hbm, gain_row), (x_hbm, x_ref), (slab_hbm, gain_slab)]
+        )
+    ]
+    for copy in small:
+        copy.start()
     load1 = pltpu.make_async_copy(w1_hbm, w1, w_sem.at[0])
     load2 = pltpu.make_async_copy(w2_hbm, w2, w_sem.at[1])
     load1.start()
     load2.start()
-
-    barrier = pltpu.get_barrier_semaphore()
-
-    def greet(i, carry):
-        pl.semaphore_signal(
-            barrier, inc=1, device_id=(peer, lax.rem(e + i, n_expert), t), device_id_type=MESH
-        )
-        return carry
-
-    lax.fori_loop(0, n_expert, greet, 0)
-    for d in range(1, n_tensor):
-        pl.semaphore_signal(
-            barrier, inc=1, device_id=(core, e, lax.rem(t + d, n_tensor)), device_id_type=MESH
-        )
 
     pad_ids[...] = jnp.full(pad_ids.shape, -1, jnp.int32)
     pad_ids[0:2, 0:tok] = ids_ref[...]
@@ -75,9 +83,13 @@
         pick = pad_ids[k:k + 1, :]
         kept = jnp.logical_and(rank < cap, pick >= 0)
         meta_send[2 + k:3 + k, :] = jnp.where(kept, pick * cap + rank, -1)
+    small[0].wait()
+    small[1].wait()
     aux_send[0:n_expert, :] = router_t[...].astype(F32)
     aux_send[n_expert:n_expert + 8, :] = jnp.broadcast_to(gain_row[...], (8, width))
 
+    small[2].wait()
+    small[3].wait()
     pl.semaphore_wait(barrier, n_expert + n_tensor - 1)
 
     meta_copy = pltpu.make_async_remote_copy(
@@ -238,6 +250,7 @@
     if slot_rows > slots:
         back[slots * half:slot_rows * half, :] = jnp.zeros(((slot_rows - slots) * half, LANES), F32)
 
+    stores = []
     for h in range(2):
         def arrive(i, carry, h=h):
             ret_copy(h, i, False).wait_recv()
@@ -252,7 +265,10 @@
         added = jnp.dot(high, table, preferred_element_type=F32)
         added = added + jnp.dot(mid, table, preferred_element_type=F32)
         added = added + jnp.dot(low, table, preferred_element_type=F32)
-        out_ref[:, cols] = (x_ref[:, cols].astype(F32) + added).astype(BF16)
+        out_ref[h] = (x_ref[:, cols].astype(F32) + added).astype(BF16)
+        store = pltpu.make_async_copy(out_ref.at[h], out_hbm.at[:, cols], out_sem.at[h])
+        store.start()
+        stores.append(store)
 
     def drain(i, carry):
         disp_copy(i).wait_send()
@@ -265,6 +281,8 @@
         return carry
 
     lax.fori_loop(0, n_expert, drain, 0)
+    for store in stores:
+        store.wait()
 
 
 def on_device(sent, norm_gain, router, w_in, w_out, expert_ids):
@@ -284,9 +302,14 @@
     result = pl.pallas_call(
         functools.partial(kernel, n_expert, n_tensor, cap, tok),
         out_shape=jax.ShapeDtypeStruct((tok, width), BF16),
-        in_specs=[vmem, vmem, vmem, vmem, vmem, hbm, hbm],
-        out_specs=vmem,
+        in_specs=[hbm, hbm, hbm, hbm, vmem, hbm, hbm],
+        out_specs=hbm,
         scratch_shapes=[
+            pltpu.VMEM((tok, width), BF16),
+            pltpu.VMEM((chunks, LANES), F32),
+            pltpu.VMEM((1, width), F32),
+            pltpu.VMEM((n_expert, width), BF16),
+            pltpu.VMEM((2, tok, width // 2), BF16),
             pltpu.VMEM((width, ff), BF16),
             pltpu.VMEM((ff, width), BF16),
             pltpu.VMEM((8, LANES), jnp.int32),
@@ -307,6 +330,8 @@
             pltpu.VMEM((2, n_expert, cap * half, LANES), BF16),
             pltpu.VMEM((2, n_expert, cap * half, LANES), BF16),
             pltpu.VMEM((slot_rows * half, LANES), F32),
+            dma((4,)),
+            dma((2,)),
             dma((2,)),
             dma((2,)),
             dma((2,)),

time: 40.9 us -> 43.2 us (1.056)
  Pallas kernels: 38.9 us -> 41.5 us
    pallas_call x1, Pallas kernels: 38.9 us -> 41.5 us  [on_device(): pl.pallas_call(functools.partial(kernel, n_expert, n_tensor, cap, tok), o...]
where the time goes in v3:
time: 43.2 us; the launch traced here: 43.1 us
  Pallas kernels  41.5 us (96%)
  local copies, waits for them, and re-layouts  1.57 us (4%)
    pallas_call x1, Pallas kernels, on_device(): pl.pallas_call(functools.partial(kernel, n_expert, n_tensor, cap, tok), o...  41.5 us
    unnamed x1, local copies, waits for them, and re-layouts  1.57 us

profile of v3, /device:TPU:1, one launch (start us, length us, event | category | flops | bytes accessed | tf_op | source)
XLA Modules:
  0.0 43.1 jit_solution(11612136528554384549)
XLA Ops:
  0.0 41.5 %expert_layer.1 = bf16[16,4096]{1,0:T(8,128)(2,1)} custom-call(bf16[16,4096]{1,0:T(8,128)(2,1)} %bitcast.14, f32[32,128]{1,0:T(8,128)} %bitcast.16, f32[1,4096]{1,0:T(1,128)} %row_hbm.1, bf16[8,4096]{1,0:T(8,128)(2,1)} %bitcast.15, s32[2,16]{1,0:T(2,128)} %bitcast.17, bf16[4096,1024]{1,0:T(8,128)(2,1)} %bitcast.11, bf16[1024,4096]{1,0:T(8,128)(2,1)} %bitcast.12), custom_call_target="tpu_custom_call" | custom-call | tf_op jit(solution)/shard_map/expert_layer/pallas_call | solution.py:302
  41.5 1.6 %copy.8 = bf16[1,16,4096]{2,1,0:T(8,128)(2,1)} copy(bf16[1,16,4096]{2,1,0:T(8,128)(2,1)} %bitcast.13) | data formatting | bytes 262144

commit v4 on v2

--- a/solution.py
+++ b/solution.py
@@ -35,8 +35,14 @@
     chunks = width // LANES
     half = chunks // 2
     slots = n_expert * cap
-    rows = n_tensor * slots
+    members = n_expert // 2
+    quarter = n_expert // 4
+    rows = n_tensor * members * cap
+    full_rows = lhs.shape[1]
     ff = w1.shape[1]
+
+    def member(g, m):
+        return (m // quarter) * (2 * quarter) + g * quarter + lax.rem(m, quarter)
 
     load1 = pltpu.make_async_copy(w1_hbm, w1, w_sem.at[0])
     load2 = pltpu.make_async_copy(w2_hbm, w2, w_sem.at[1])
@@ -114,50 +120,56 @@
             device_id=(core, e, lax.rem(t + d, n_tensor)), device_id_type=MESH,
         )
 
-    def send_disp(i, carry):
-        disp_copy(i).start()
-        return carry
-
-    lax.fori_loop(0, n_expert, send_disp, 0)
-
-    def normalise(d, i):
-        piece = got[d, i].astype(F32).reshape(cap, chunks, LANES)
+    for g in range(2):
+        def send_disp(m, carry, g=g):
+            disp_copy(member(g, m)).start()
+            return carry
+
+        lax.fori_loop(0, members, send_disp, 0)
+
+    if full_rows > rows:
+        for g in range(2):
+            flat[g, rows * chunks:full_rows * chunks, :] = jnp.zeros(((full_rows - rows) * chunks, LANES), F32)
+
+    def normalise(g, d, m):
+        piece = got[d, member(g, m)].astype(F32).reshape(cap, chunks, LANES)
         total = jnp.sum(jnp.sum(piece * piece, axis=1, keepdims=True), axis=2, keepdims=True)
         scale = lax.rsqrt(total * (1.0 / width) + 1e-05)
         normed = (piece * scale * gain_slab[...][None]).astype(BF16).astype(F32)
-        start = pl.multiple_of((d * n_expert + i) * (cap * chunks), cap * chunks)
-        flat[pl.ds(start, cap * chunks), :] = normed.reshape(cap * chunks, LANES)
-
-    def take(i, carry):
-        disp_copy(i).wait_recv()
+        start = pl.multiple_of((d * members + m) * (cap * chunks), cap * chunks)
+        flat[g, pl.ds(start, cap * chunks), :] = normed.reshape(cap * chunks, LANES)
+
+    def take(g):
+        def one(m, carry):
+            disp_copy(member(g, m)).wait_recv()
+            for d in range(1, n_tensor):
+                fwd_copy(d, member(g, m), True).start()
+            normalise(g, 0, m)
+            return carry
+
+        lax.fori_loop(0, members, one, 0)
+
+    def take_forwarded(g):
         for d in range(1, n_tensor):
-            fwd_copy(d, i, True).start()
-        normalise(0, i)
-        return carry
-
-    lax.fori_loop(0, n_expert, take, 0)
-    for d in range(1, n_tensor):
-        def take_fwd(i, carry, d=d):
-            fwd_copy(d, i, False).wait_recv()
-            normalise(d, i)
-            return carry
-
-        lax.fori_loop(0, n_expert, take_fwd, 0)
-
-    for c in range(chunks):
-        lhs[:, c * LANES:(c + 1) * LANES] = flat[pl.ds(c, rows, stride=chunks), :].astype(BF16)
+            def one(m, carry, d=d):
+                fwd_copy(d, member(g, m), False).wait_recv()
+                normalise(g, d, m)
+                return carry
+
+            lax.fori_loop(0, members, one, 0)
+        for c in range(chunks):
+            lhs[g, :, c * LANES:(c + 1) * LANES] = flat[g, pl.ds(c, full_rows, stride=chunks), :].astype(BF16)
 
     tile = 256
-    load1.wait()
-
-    def first(n, carry):
-        cols = pl.ds(pl.multiple_of(n * tile, tile), tile)
-        value = jnp.dot(lhs[...], w1[:, cols], preferred_element_type=F32)
-        hid[:, cols] = jax.nn.gelu(value).astype(BF16)
-        return carry
-
-    lax.fori_loop(0, ff // tile, first, 0)
-    load2.wait()
+
+    def first(g):
+        def one(n, carry):
+            cols = pl.ds(pl.multiple_of(n * tile, tile), tile)
+            value = jnp.dot(lhs[g], w1[:, cols], preferred_element_type=F32)
+            hid[g, :, cols] = jax.nn.gelu(value).astype(BF16)
+            return carry
+
+        lax.fori_loop(0, ff // tile, one, 0)
 
     def part_copy(h, d, i, sending):
         there = (n_tensor - d) if sending else d
@@ -176,32 +188,34 @@
 
     piece_rows = cap * half
 
-    for h in range(2):
-        def second(n, carry, h=h):
+    def second(g, h):
+        def one(n, carry):
             cols = pl.ds(pl.multiple_of(h * half * LANES + n * tile, tile), tile)
-            value = jnp.dot(hid[...], w2[:, cols], preferred_element_type=F32)
+            value = jnp.dot(hid[g], w2[:, cols], preferred_element_type=F32)
             for j in range(tile // LANES):
-                partial[h, pl.ds(n * (tile // LANES) + j, rows, stride=half), :] = (
-                    value[:, j * LANES:(j + 1) * LANES]
+                partial[g, h, pl.ds(n * (tile // LANES) + j, rows, stride=half), :] = (
+                    value[0:rows, j * LANES:(j + 1) * LANES]
                 )
             return carry
 
-        lax.fori_loop(0, half * LANES // tile, second, 0)
+        lax.fori_loop(0, half * LANES // tile, one, 0)
         for d in range(1, n_tensor):
-            def send_part(k, carry, h=h, d=d):
-                i = n_expert - 1 - k
-                start = pl.multiple_of((d * n_expert + i) * piece_rows, piece_rows)
-                part_send[h, d, i] = partial[h, pl.ds(start, piece_rows), :].astype(BF16)
+            def send_part(k, carry, d=d):
+                m = members - 1 - k
+                i = member(g, m)
+                start = pl.multiple_of((d * members + m) * piece_rows, piece_rows)
+                part_send[h, d, i] = partial[g, h, pl.ds(start, piece_rows), :].astype(BF16)
                 part_copy(h, d, i, True).start()
                 return carry
 
-            lax.fori_loop(0, n_expert, send_part, 0)
-
-    def reduce(h):
+            lax.fori_loop(0, members, send_part, 0)
+
+    def reduce(g, h):
         def one(k, carry):
-            i = n_expert - 1 - k
-            start = pl.multiple_of(i * piece_rows, piece_rows)
-            total = partial[h, pl.ds(start, piece_rows), :].astype(BF16).astype(F32)
+            m = members - 1 - k
+            i = member(g, m)
+            start = pl.multiple_of(m * piece_rows, piece_rows)
+            total = partial[g, h, pl.ds(start, piece_rows), :].astype(BF16).astype(F32)
             for d in range(1, n_tensor):
                 part_copy(h, d, i, False).wait_recv()
                 total = total + part_recv[h, d, i].astype(F32)
@@ -209,10 +223,24 @@
             ret_copy(h, i, True).start()
             return carry
 
-        lax.fori_loop(0, n_expert, one, 0)
-
-    reduce(0)
-    reduce(1)
+        lax.fori_loop(0, members, one, 0)
+
+    take(0)
+    take_forwarded(0)
+    load1.wait()
+    first(0)
+    take(1)
+    load2.wait()
+    second(0, 0)
+    second(0, 1)
+    take_forwarded(1)
+    reduce(0, 0)
+    first(1)
+    reduce(0, 1)
+    second(1, 0)
+    second(1, 1)
+    reduce(1, 0)
+    reduce(1, 1)
 
     aux_copy.wait()
     x_f = x_ref[...].astype(F32)
@@ -275,7 +303,8 @@
     cap = max(2, (5 * top * tok + 4 * n_expert - 1) // (4 * n_expert))
     slots = n_expert * cap
     slot_rows = -(-slots // 16) * 16
-    rows = n_tensor * slots
+    rows = n_tensor * slots // 2
+    full_rows = -(-rows // 16) * 16
     chunks = width // LANES
     half = chunks // 2
     vmem = pl.BlockSpec(memory_space=pltpu.VMEM)
@@ -298,10 +327,10 @@
             pltpu.VMEM((slots * chunks, LANES), F32),
             pltpu.VMEM((n_expert, cap * chunks, LANES), BF16),
             pltpu.VMEM((n_tensor, n_expert, cap * chunks, LANES), BF16),
-            pltpu.VMEM((rows * chunks, LANES), F32),
-            pltpu.VMEM((rows, width), BF16),
-            pltpu.VMEM((rows, ff), BF16),
-            pltpu.VMEM((2, rows * half, LANES), F32),
+            pltpu.VMEM((2, full_rows * chunks, LANES), F32),
+            pltpu.VMEM((2, full_rows, width), BF16),
+            pltpu.VMEM((2, full_rows, ff), BF16),
+            pltpu.VMEM((2, 2, rows * half, LANES), F32),
             pltpu.VMEM((2, n_tensor, n_expert, cap * half, LANES), BF16),
             pltpu.VMEM((2, n_tensor, n_expert, cap * half, LANES), BF16),
             pltpu.VMEM((2, n_expert, cap * half, LANES), BF16),

time: 40.9 us -> 44 us (1.076)
  Pallas kernels: 38.9 us -> 42.3 us
    pallas_call x1, Pallas kernels: 38.9 us -> 42.3 us  [on_device(): pl.pallas_call(functools.partial(kernel, n_expert, n_tensor, cap, tok), o...]
where the time goes in v4:
time: 44 us; the launch traced here: 43.9 us
  Pallas kernels  42.3 us (96%)
  local copies, waits for them, and re-layouts  1.57 us (4%)
    pallas_call x1, Pallas kernels, on_device(): pl.pallas_call(functools.partial(kernel, n_expert, n_tensor, cap, tok), o...  42.3 us
    unnamed x1, local copies, waits for them, and re-layouts  1.57 us

profile of v4, /device:TPU:1, one launch (start us, length us, event | category | flops | bytes accessed | tf_op | source)
XLA Modules:
  0.0 43.9 jit_solution(15768415606125911496)
XLA Ops:
  0.0 42.3 %expert_layer.1 = bf16[16,4096]{1,0:T(8,128)(2,1)} custom-call(bf16[16,4096]{1,0:T(8,128)(2,1)} %bitcast.14, f32[32,128]{1,0:T(8,128)} %bitcast.16, f32[1,4096]{1,0:T(1,128)} %gain_row.1, bf16[8,4096]{1,0:T(8,128)(2,1)} %bitcast.15, s32[2,16]{1,0:T(2,128)} %bitcast.17, bf16[4096,1024]{1,0:T(8,128)(2,1)} %bitcast.11, bf16[1024,4096]{1,0:T(8,128)(2,1)} %bitcast.12), custom_call_target="tpu_custom_call" | custom-call | tf_op jit(solution)/shard_map/expert_layer/pallas_call | solution.py:313
  42.3 1.6 %copy.8 = bf16[1,16,4096]{2,1,0:T(8,128)(2,1)} copy(bf16[1,16,4096]{2,1,0:T(8,128)(2,1)} %bitcast.13) | data formatting | bytes 262144
